TPU v7x, 32 devices: a whole 2x2x4 slice. The times are simulated.
32 devices in a mesh: hi: 4 (over x, core), lo: 8 (over z, y).
Axes of the slice: x: 2, y: 2, z: 4, core: 2. Of those that a mesh axis runs over, the one named last changes fastest.
Arguments:
- blocks: bfloat16 [2048, 128, 128], P(('hi', 'lo')), may hold values from -6 to 6
- diag_factors: bfloat16 [4, 2048, 128, 128], P(None, ('hi', 'lo')), may hold values from -0.375 to 0.375
- off_factors: bfloat16 [4, 2048, 128, 128], P(None, ('hi', 'lo')), may hold values from -0.375 to 0.375
- partner_maps: int32 [4, 64], replicated, may hold values from 0 to 63, each once within a row
Outputs:
- summed: bfloat16 [512, 128, 128], P(('lo', 'hi'))
Inputs may be any that keep to these rules, and one draw needn't show every extreme that they name: Each row of partner_maps is a permutation of 0 to 63.
All inputs are finite; a program needn't handle non-finite values.
Results may differ from a plain program's by a relative error of at most 0.009.
Values may be sent and summed in bfloat16 or wider, within the bound.
A program may use at most 128 MiB of HBM per device.

v0:
```python
import jax
import jax.numpy as jnp
from jax import lax
from jax.sharding import PartitionSpec as P


def partner_2(array, axis, apart):
    return lax.ppermute(array, axis, [(i, i ^ 1 << apart) for i in range(lax.axis_size(axis))])


def apply_factor(factor, data):
    return jnp.einsum("bij,brj->bri", factor, data, preferred_element_type=jnp.float32)


def body(blocks, diag_factors, off_factors, partner_maps):
    current = blocks
    top = lax.axis_size("lo").bit_length() - 1
    for level, bit in enumerate((0, 1, top - 1)):
        partner = partner_2(current, "lo", bit)
        partner = jnp.take(partner, partner_maps[level], axis=0)
        mixed = apply_factor(diag_factors[level], current) + apply_factor(
            off_factors[level], partner
        )
        current = mixed.astype(jnp.bfloat16)
    own = apply_factor(diag_factors[3], current)
    moved = apply_factor(off_factors[3], current)
    moved = partner_2(moved.astype(jnp.bfloat16), "hi", 1).astype(moved.dtype)
    local = own + jnp.take(moved, partner_maps[3], axis=0)
    whole = lax.psum(local, "hi")
    count = local.shape[0] // lax.axis_size("hi")
    share = lax.dynamic_slice_in_dim(whole, lax.axis_index("hi") * count, count, 0)
    return share.astype(jnp.bfloat16)


def solution(mesh):
    in_specs = (
        P(("hi", "lo"), None, None),
        P(None, ("hi", "lo"), None, None),
        P(None, ("hi", "lo"), None, None),
        P(),
    )
    out_specs = P(("lo", "hi"), None, None)
    return jax.shard_map(body, mesh=mesh, in_specs=in_specs, out_specs=out_specs, check_vma=False)
```

profile of v0, /device:TPU:0, one launch (start us, length us, event | category | flops | bytes accessed | tf_op | source)
XLA Modules:
  0.0 352.7 jit_solution(16989060003939846551)
XLA Ops:
  0.0 3.0 collective-permute-start
  3.0 0.8 compare_and_fusion
  3.8 5.7 %fusion.11 = f32[64,128,128]{2,1,0:T(8,128)} fusion(bf16[64,128,128]{2,1,0:T(8,128)(2,1)} %param.6, bf16[4,64,128,128]{3,2,1,0:T(8,128)(2,1)} %param.7), kind=kOutput, calls=%fused_computation.19 | convolution fusion | flops 268435456 | bytes 8388608 | tf_op jit(solution)/shard_map/bij,brj->bri/dot_general | solution.py:12
  9.6 39.4 %collective-permute-done = bf16[64,128,128]{2,1,0:T(8,128)(2,1)} collective-permute-done((bf16[64,128,128]{2,1,0:T(8,128)(2,1)}, bf16[64,128,128]{2,1,0:T(8,128)(2,1)}, u32[]{:S(2)}, u32[]{:S(2)}) %collective-permute-start) | collective-permute-done | bytes 2097184 | tf_op jit(solution)/shard_map/ppermute | solution.py:8
  48.9 2.5 gather_fusion.1
  51.5 4.5 %add_convert_fusion.2 = bf16[64,128,128]{2,1,0:T(8,128)(2,1)S(1)} fusion(f32[64,128,128]{2,1,0:T(8,128)} %fusion.11, bf16[64,128,128]{2,1,0:T(8,128)(2,1)S(1)} %gather_fusion.1, bf16[4,64,128,128]{3,2,1,0:T(8,128)(2,1)} %param.8, pred[64]{0:T(512)(128)(4,1)S(1)} %get-tuple-element.16), kind=kOutput, calls=%fused_computation.7 | convolution fusion | flops 271581184 | bytes 10485824 | tf_op jit(solution)/shard_map/bij,brj->bri/dot_general | solution.py:12
  55.9 1.9 collective-permute-start.1
  57.8 5.1 %fusion.8 = f32[64,128,128]{2,1,0:T(8,128)} fusion(bf16[64,128,128]{2,1,0:T(8,128)(2,1)S(1)} %add_convert_fusion.2, bf16[4,64,128,128]{3,2,1,0:T(8,128)(2,1)} %param.7), kind=kOutput, calls=%fused_computation.16 | convolution fusion | flops 268435456 | bytes 8388608 | tf_op jit(solution)/shard_map/bij,brj->bri/dot_general | solution.py:12
  62.9 40.0 %collective-permute-done.1 = bf16[64,128,128]{2,1,0:T(8,128)(2,1)} collective-permute-done((bf16[64,128,128]{2,1,0:T(8,128)(2,1)S(1)}, bf16[64,128,128]{2,1,0:T(8,128)(2,1)}, u32[]{:S(2)}, u32[]{:S(2)}) %collective-permute-start.1) | collective-permute-done | bytes 2097184 | tf_op jit(solution)/shard_map/ppermute | solution.py:8
  102.9 2.5 gather_fusion.2
  105.4 4.4 %add_convert_fusion.1 = bf16[64,128,128]{2,1,0:T(8,128)(2,1)S(1)} fusion(f32[64,128,128]{2,1,0:T(8,128)} %fusion.8, bf16[64,128,128]{2,1,0:T(8,128)(2,1)S(1)} %gather_fusion.2, bf16[4,64,128,128]{3,2,1,0:T(8,128)(2,1)} %param.8, pred[64]{0:T(512)(128)(4,1)S(1)} %get-tuple-element.14), kind=kOutput, calls=%fused_computation.6 | convolution fusion | flops 271581184 | bytes 10485824 | tf_op jit(solution)/shard_map/bij,brj->bri/dot_general | solution.py:12
  109.9 2.6 collective-permute-start.2
  112.5 5.1 %fusion.5 = f32[64,128,128]{2,1,0:T(8,128)} fusion(bf16[64,128,128]{2,1,0:T(8,128)(2,1)S(1)} %add_convert_fusion.1, bf16[4,64,128,128]{3,2,1,0:T(8,128)(2,1)} %param.7), kind=kOutput, calls=%fused_computation.13 | convolution fusion | flops 268435456 | bytes 8388608 | tf_op jit(solution)/shard_map/bij,brj->bri/dot_general | solution.py:12
  117.6 84.1 %collective-permute-done.2 = bf16[64,128,128]{2,1,0:T(8,128)(2,1)S(1)} collective-permute-done((bf16[64,128,128]{2,1,0:T(8,128)(2,1)S(1)}, bf16[64,128,128]{2,1,0:T(8,128)(2,1)S(1)}, u32[]{:S(2)}, u32[]{:S(2)}) %collective-permute-start.2) | collective-permute-done | bytes 2097184 | tf_op jit(solution)/shard_map/ppermute | solution.py:8
  201.7 2.1 gather_fusion.3
  203.8 5.1 %add_convert_fusion = bf16[64,128,128]{2,1,0:T(8,128)(2,1)S(1)} fusion(f32[64,128,128]{2,1,0:T(8,128)} %fusion.5, bf16[64,128,128]{2,1,0:T(8,128)(2,1)} %gather_fusion.3, bf16[4,64,128,128]{3,2,1,0:T(8,128)(2,1)} %param.8, pred[64]{0:T(512)(128)(4,1)S(1)} %get-tuple-element.6), kind=kOutput, calls=%fused_computation.5 | convolution fusion | flops 271581184 | bytes 10485824 | tf_op jit(solution)/shard_map/bij,brj->bri/dot_general | solution.py:12
  208.9 4.5 %fusion.27 = bf16[64,128,128]{2,1,0:T(8,128)(2,1)} fusion(bf16[64,128,128]{2,1,0:T(8,128)(2,1)S(1)} %add_convert_fusion, bf16[4,64,128,128]{3,2,1,0:T(8,128)(2,1)} %param.8), kind=kOutput, calls=%fused_computation.35 | convolution fusion | flops 269484032 | bytes 6291456 | tf_op jit(solution)/shard_map/bij,brj->bri/dot_general | solution.py:12
  213.4 1.1 collective-permute-start.3
  214.5 0.7 fusion.33
  215.2 5.1 %fusion.2 = f32[64,128,128]{2,1,0:T(8,128)} fusion(bf16[64,128,128]{2,1,0:T(8,128)(2,1)S(1)} %add_convert_fusion, bf16[4,64,128,128]{3,2,1,0:T(8,128)(2,1)} %param.7), kind=kOutput, calls=%fused_computation.10 | convolution fusion | flops 268435456 | bytes 8388608 | tf_op jit(solution)/shard_map/bij,brj->bri/dot_general | solution.py:12
  220.3 40.3 %collective-permute-done.3 = bf16[64,128,128]{2,1,0:T(8,128)(2,1)} collective-permute-done((bf16[64,128,128]{2,1,0:T(8,128)(2,1)}, bf16[64,128,128]{2,1,0:T(8,128)(2,1)}, u32[]{:S(2)}, u32[]{:S(2)}) %collective-permute-start.3) | collective-permute-done | bytes 2097184 | tf_op jit(solution)/shard_map/ppermute | solution.py:8
  260.6 4.1 %convert_element_type.22 = f32[64,128,128]{2,1,0:T(8,128)} convert(bf16[64,128,128]{2,1,0:T(8,128)(2,1)} %collective-permute-done.3) | non-fusion elementwise | flops 1048576 | bytes 6291456 | tf_op jit(solution)/shard_map/convert_element_type | solution.py:27
  264.7 5.0 %gather_fusion = f32[64,128,128]{2,1,0:T(8,128)} fusion(f32[64,128,128]{2,1,0:T(8,128)} %convert_element_type.22, s32[1024]{0:T(1024)S(1)} %pad_clamp_fusion), kind=kCustom, calls=%fused_computation.3 | custom fusion | bytes 8388864 | tf_op jit(solution)/shard_map/jit(_take)/gather | solution.py:28
  269.7 5.9 %select_add_fusion = f32[64,128,128]{2,1,0:T(8,128)} fusion(f32[64,128,128]{2,1,0:T(8,128)} %fusion.2, f32[64,128,128]{2,1,0:T(8,128)} %gather_fusion, pred[64]{0:T(512)(128)(4,1)S(1)} %get-tuple-element.13), kind=kLoop, calls=%fused_computation.4 | loop fusion | flops 2097152 | bytes 12582976 | tf_op jit(solution)/shard_map/add | solution.py:28
  275.5 76.3 %all-reduce.1 = bf16[64,128,128]{2,1,0:T(8,128)(2,1)S(1)} all-reduce(f32[64,128,128]{2,1,0:T(8,128)} %select_add_fusion), channel_id=1, replica_groups=mesh['hi'=4,'lo'=8] {'hi'}, use_global_device_ids=true, to_apply=%region_0.0 | all-reduce | flops 1048576 | bytes 6291456 | tf_op jit(solution)/shard_map/psum | solution.py:29
  351.8 0.8 dynamic-slice_convert_fusion
  (4 shorter events, 0.0 us)
Async XLA Ops:
  0.0 48.9 %collective-permute-start = (bf16[64,128,128]{2,1,0:T(8,128)(2,1)}, bf16[64,128,128]{2,1,0:T(8,128)(2,1)}, u32[]{:S(2)}, u32[]{:S(2)}) collective-permute-start(bf16[64,128,128]{2,1,0:T(8,128)(2,1)} %param.6), channel_id=1, source_target_pairs={{0,1},{1,0},{2,3},{3,2},{4,5},{5,4},{6,7},{7,6},{8,9},{9,8},{10,11... | collective-permute-start | bytes 6291464 | tf_op jit(solution)/shard_map/ppermute | solution.py:8
  55.9 47.0 %collective-permute-start.1 = (bf16[64,128,128]{2,1,0:T(8,128)(2,1)S(1)}, bf16[64,128,128]{2,1,0:T(8,128)(2,1)}, u32[]{:S(2)}, u32[]{:S(2)}) collective-permute-start(bf16[64,128,128]{2,1,0:T(8,128)(2,1)S(1)} %add_convert_fusion.2), channel_id=1, source_target_pairs={{0,2},{1,3},{2,0},{3,1},{4,6},{5,7},{6,4},{7,5},{8,10},{9,11},{10,... | collective-permute-start | bytes 6291464 | tf_op jit(solution)/shard_map/ppermute | solution.py:8
  109.9 91.8 %collective-permute-start.2 = (bf16[64,128,128]{2,1,0:T(8,128)(2,1)S(1)}, bf16[64,128,128]{2,1,0:T(8,128)(2,1)S(1)}, u32[]{:S(2)}, u32[]{:S(2)}) collective-permute-start(bf16[64,128,128]{2,1,0:T(8,128)(2,1)S(1)} %add_convert_fusion.1), channel_id=1, source_target_pairs={{0,4},{1,5},{2,6},{3,7},{4,0},{5,1},{6,2},{7,3},{8,12},{9,13},{10,... | collective-permute-start | bytes 6291464 | tf_op jit(solution)/shard_map/ppermute | solution.py:8
  213.4 47.2 %collective-permute-start.3 = (bf16[64,128,128]{2,1,0:T(8,128)(2,1)}, bf16[64,128,128]{2,1,0:T(8,128)(2,1)}, u32[]{:S(2)}, u32[]{:S(2)}) collective-permute-start(bf16[64,128,128]{2,1,0:T(8,128)(2,1)} %fusion.27), channel_id=1, source_target_pairs={{0,16},{8,24},{16,0},{24,8},{1,17},{9,25},{17,1},{25,9},{2,18},{10... | collective-permute-start | bytes 6291464 | tf_op jit(solution)/shard_map/ppermute | solution.py:8
where the time goes:
time: 353 us
  waiting for transfers between devices  204 us (58%)
  blocking collectives  76.3 us (22%)
  matrix products  39.5 us (11%)
  local copies, waits for them, and re-layouts  13 us (4%)
  other arithmetic  11.5 us (3%)
  starting transfers between devices  8.47 us (2%)
    ppermute x4, waiting for transfers between devices, partner_2(): lax.ppermute(array, axis, [(i, i ^ 1 << apart) for i in range(lax.axis_si...  204 us
    psum x1, blocking collectives, body(): whole = lax.psum(local, 'hi')  76.3 us
    dot_general x8, matrix products, apply_factor(): jnp.einsum('bij,brj->bri', factor, data, preferred_element_type=jnp.float32)  39.5 us
    ppermute x4, starting transfers between devices, partner_2(): lax.ppermute(array, axis, [(i, i ^ 1 << apart) for i in range(lax.axis_si...  8.47 us
    gather x3, local copies, waits for them, and re-layouts, body(): partner = jnp.take(partner, partner_maps[level], axis=0)  7.21 us
  transfers between devices with their start and end apart: 4, of which 4 were waited for; matrix products, arithmetic and copies ran while one was open for 6% of the time, Pallas kernels for 0%

commit v1 on v0

v1 whole, which is shorter than its diff:
```python
import functools

import jax
import jax.numpy as jnp
from jax import lax
from jax.experimental import pallas as pl
from jax.experimental.pallas import tpu as pltpu
from jax.sharding import PartitionSpec as P

MESH = pl.DeviceIdType.MESH
UNROLL = 8


def chunk_plan(rows):
    unit = rows // 8
    sizes = (unit, 2 * unit, 2 * unit, 2 * unit, unit)
    starts = [sum(sizes[:i]) for i in range(len(sizes))]
    return tuple(zip(starts, sizes))


def order_of(chunks):
    y_free = z_free = mid_free = 0.0
    times = []
    for c, (_, size) in enumerate(chunks):
        y_free = y_free + size
        times.append((y_free, 0, c))
        z_free = max(z_free, y_free) + size * (1.0 if c == 0 else 1.5)
        times.append((z_free, 1, c))
        mid_free = max(mid_free, z_free) + 2 * size
        times.append((mid_free, 2, c))
    return [(level, c) for _, level, c in sorted(times)]


def flip(index, step):
    return index + step * (1 - 2 * (lax.rem(lax.div(index, step), 2)))


def kernel(n_hi, n_lo, chunks, maps, blocks, diag, off, out, *scratch):
    count = len(chunks)
    scratch = list(scratch)

    def take(number):
        taken = scratch[:number]
        del scratch[:number]
        return taken

    x0, = take(1)
    xs = [None] + [take(count) for _ in range(3)]
    recv = [take(count) for _ in range(3)]
    partial = take(count)
    others = take(count)
    dfs = take(4)
    ofs = take(4)
    load_sem, factor_sem, send_sem, recv_sem, sum_send, sum_recv = scratch

    hi = lax.axis_index("hi")
    lo = lax.axis_index("lo")
    steps = (1, 2, n_lo // 2)
    nblk = blocks.shape[0]
    share = nblk // n_hi

    near = sorted(set(steps))
    lo_partner = {s: flip(lo, s) for s in near}
    hi_partner = [lax.rem(hi + d, n_hi) for d in range(1, n_hi)]
    barrier = pltpu.get_barrier_semaphore()
    for s in near:
        pl.semaphore_signal(barrier, inc=1, device_id=(hi, lo_partner[s]), device_id_type=MESH)
    for h in hi_partner:
        pl.semaphore_signal(barrier, inc=1, device_id=(h, lo), device_id_type=MESH)

    load_x = pltpu.make_async_copy(blocks, x0, load_sem)
    load_x.start()
    loads = []
    for k in range(4):
        loads.append((
            pltpu.make_async_copy(diag.at[k], dfs[k], factor_sem.at[0, k]),
            pltpu.make_async_copy(off.at[k], ofs[k], factor_sem.at[1, k]),
        ))
    for copy in loads[0]:
        copy.start()
    pl.semaphore_wait(barrier, len(near) + n_hi - 1)

    def exchange(level, c):
        start, size = chunks[c]
        source = blocks.at[:, pl.ds(start, size), :] if level == 0 else xs[level][c]
        return pltpu.make_async_remote_copy(
            src_ref=source,
            dst_ref=recv[level][c],
            send_sem=send_sem.at[level, c],
            recv_sem=recv_sem.at[level, c],
            device_id=(hi, lo_partner[steps[level]]),
            device_id_type=MESH,
        )

    def hand_on(c, d):
        return pltpu.make_async_remote_copy(
            src_ref=partial[c].at[pl.ds(hi_partner[d] * share, share)],
            dst_ref=others[c].at[d],
            send_sem=sum_send.at[d, c],
            recv_sem=sum_recv.at[d, c],
            device_id=(hi_partner[d], lo),
            device_id_type=MESH,
        )

    def product(left, right, d, o):
        return lax.dot_general(
            jnp.concatenate([left, right], axis=1),
            jnp.concatenate([d, o], axis=1),
            (((1,), (1,)), ((), ())),
            preferred_element_type=jnp.float32,
        ).astype(jnp.bfloat16)

    def over_blocks(number, one):
        unroll = UNROLL if number % UNROLL == 0 else 1

        def some(i, _):
            for u in range(unroll):
                one(i * unroll + u)
            return 0

        lax.fori_loop(0, number // unroll, some, 0)

    def mix(level, c):
        start, size = chunks[c]

        def one(j):
            mine = x0[j, pl.ds(start, size), :] if level == 0 else xs[level][c][j]
            theirs = recv[level][c][maps[level, j]]
            xs[level + 1][c][j] = product(mine, theirs, dfs[level][j], ofs[level][j])

        over_blocks(nblk, one)

    def last(c):
        def one(j):
            p = maps[3, j]
            partial[c][j] = product(xs[3][c][j], xs[3][c][p], dfs[3][j], ofs[3][p])

        over_blocks(nblk, one)

    def gather_sum(c):
        start, size = chunks[c]
        for d in range(n_hi - 1):
            hand_on(c, d).wait_recv()

        def one(i):
            total = partial[c][hi * share + i].astype(jnp.float32)
            for d in range(n_hi - 1):
                total = total + others[c][d, i].astype(jnp.float32)
            out[i, pl.ds(start, size), :] = total.astype(jnp.bfloat16)

        over_blocks(share, one)

    exchange(0, 0).start()
    for k in range(1, 4):
        for copy in loads[k]:
            copy.start()
    load_x.wait()
    loaded = set()
    pending = []
    for level, c in order_of(chunks):
        exchange(level, c).wait_recv()
        if level == 0 and c + 1 < count:
            exchange(0, c + 1).start()
        if level not in loaded:
            for copy in loads[level]:
                copy.wait()
            loaded.add(level)
        mix(level, c)
        if level < 2:
            exchange(level + 1, c).start()
            continue
        if 3 not in loaded:
            for copy in loads[3]:
                copy.wait()
            loaded.add(3)
        last(c)
        for d in range(n_hi - 1):
            hand_on(c, d).start()
        for earlier in pending:
            gather_sum(earlier)
        pending = [c]
    for earlier in pending:
        gather_sum(earlier)
    for c in range(count):
        for level in range(3):
            exchange(level, c).wait_send()
        for d in range(n_hi - 1):
            hand_on(c, d).wait_send()


def body(n_hi, n_lo, blocks, diag_factors, off_factors, partner_maps):
    nblk, rows, width = blocks.shape
    chunks = chunk_plan(rows)
    count = len(chunks)
    share = nblk // n_hi
    bf16 = jnp.bfloat16
    whole = pltpu.VMEM((nblk, rows, width), bf16)
    pieces = [pltpu.VMEM((nblk, size, width), bf16) for _, size in chunks]
    shares = [pltpu.VMEM((n_hi - 1, share, size, width), bf16) for _, size in chunks]
    factor = pltpu.VMEM((nblk, width, width), bf16)
    return pl.pallas_call(
        functools.partial(kernel, n_hi, n_lo, chunks),
        out_shape=jax.ShapeDtypeStruct((share, rows, width), bf16),
        in_specs=[pl.BlockSpec(memory_space=pltpu.SMEM)] + [pl.BlockSpec(memory_space=pl.ANY)] * 3,
        out_specs=pl.BlockSpec(memory_space=pltpu.VMEM),
        scratch_shapes=[whole] + pieces * 7 + shares + [factor] * 8 + [
            pltpu.SemaphoreType.DMA,
            pltpu.SemaphoreType.DMA((2, 4)),
            pltpu.SemaphoreType.DMA((3, count)),
            pltpu.SemaphoreType.DMA((3, count)),
            pltpu.SemaphoreType.DMA((n_hi - 1, count)),
            pltpu.SemaphoreType.DMA((n_hi - 1, count)),
        ],
        compiler_params=pltpu.CompilerParams(
            collective_id=0, has_side_effects=True, vmem_limit_bytes=56 * 1024 * 1024
        ),
        cost_estimate=pl.CostEstimate(
            flops=16 * nblk * rows * width * width,
            bytes_accessed=2 * (blocks.size + 8 * nblk * width * width + share * rows * width),
            transcendentals=0,
        ),
    )(partner_maps, blocks, diag_factors, off_factors)


def solution(mesh):
    in_specs = (
        P(("hi", "lo"), None, None),
        P(None, ("hi", "lo"), None, None),
        P(None, ("hi", "lo"), None, None),
        P(),
    )
    out_specs = P(("lo", "hi"), None, None)
    run = functools.partial(body, mesh.shape["hi"], mesh.shape["lo"])
    return jax.shard_map(run, mesh=mesh, in_specs=in_specs, out_specs=out_specs, check_vma=False)
```

time: 353 us -> 140 us (0.40)
  waiting for transfers between devices: 204 us -> 0 us
  Pallas kernels: 0 us -> 138 us
  blocking collectives: 76.3 us -> 0 us
  matrix products: 39.5 us -> 0 us
  other arithmetic: 11.5 us -> 0 us
  local copies, waits for them, and re-layouts: 13 us -> 1.89 us
  starting transfers between devices: 8.47 us -> 0 us
    ppermute x4 -> x0, waiting for transfers between devices: 204 us -> none  [partner_2(): lax.ppermute(array, axis, [(i, i ^ 1 << apart) for i in range(lax.axis_si...]
    pallas_call x0 -> x1, Pallas kernels: none -> 138 us  [body(): pl.pallas_call(functools.partial(kernel, n_hi, n_lo, chunks), out_shape=j...]
    psum x1 -> x0, blocking collectives: 76.3 us -> none  [body(): whole = lax.psum(local, 'hi')]
    dot_general x8 -> x0, matrix products: 39.5 us -> none  [apply_factor(): jnp.einsum('bij,brj->bri', factor, data, preferred_element_type=jnp.float32)]
    gather x4 -> x0, local copies, waits for them, and re-layouts: 12.2 us -> none  [the longest x3 7.21 us: body(): partner = jnp.take(partner, partner_maps[level], axis=0)]
    ppermute x4 -> x0, starting transfers between devices: 8.47 us -> none  [partner_2(): lax.ppermute(array, axis, [(i, i ^ 1 << apart) for i in range(lax.axis_si...]
    add x1 -> x0, other arithmetic: 5.87 us -> none  [body(): local = own + jnp.take(moved, partner_maps[3], axis=0)]
    convert_element_type x1 -> x0, other arithmetic: 4.07 us -> none  [body(): moved = partner_2(moved.astype(jnp.bfloat16), 'hi', 1).astype(moved.dtype)]
  transfers between devices with their start and end apart: 4 -> 0, of which waited for: 4 -> 0; matrix products, arithmetic and copies ran while one was open for 6% -> 0% of each run, Pallas kernels for 0% -> 0%
where the time goes in v1:
time: 140 us
  Pallas kernels  138 us (99%)
  local copies, waits for them, and re-layouts  1.89 us (1%)
    pallas_call x1, Pallas kernels, body(): pl.pallas_call(functools.partial(kernel, n_hi, n_lo, chunks), out_shape=j...  138 us

profile of v1, /device:TPU:0, one launch (start us, length us, event | category | flops | bytes accessed | tf_op | source)
XLA Modules:
  0.0 140.1 jit_solution(1276717890342030178)
XLA Ops:
  0.0 138.2 %shard_map.46 = bf16[16,128,128]{2,1,0:T(8,128)(2,1)} custom-call(s32[4,64]{1,0:T(4,128)} %maps.1, bf16[64,128,128]{2,1,0:T(8,128)(2,1)} %blocks.1, bf16[4,64,128,128]{3,2,1,0:T(8,128)(2,1)} %diag.1, bf16[4,64,128,128]{3,2,1,0:T(8,128)(2,1)} %off.1), custom_call_target="tpu_custom_call" | custom-call | flops 2147483648 | bytes 19398656 | tf_op jit(solution)/shard_map/pallas_call | solution.py:201
  138.2 1.9 %copy.6 = bf16[16,128,128]{2,1,0:T(8,128)(2,1)} copy(bf16[16,128,128]{2,1,0:T(8,128)(2,1)} %shard_map.46) | data formatting | bytes 1048576

commit v2 on v1

--- a/solution.py
+++ b/solution.py
@@ -8,27 +8,25 @@
 from jax.sharding import PartitionSpec as P
 
 MESH = pl.DeviceIdType.MESH
-UNROLL = 8
+UNROLL = 16
 
 
 def chunk_plan(rows):
-    unit = rows // 8
-    sizes = (unit, 2 * unit, 2 * unit, 2 * unit, unit)
-    starts = [sum(sizes[:i]) for i in range(len(sizes))]
-    return tuple(zip(starts, sizes))
-
-
-def order_of(chunks):
-    y_free = z_free = mid_free = 0.0
-    times = []
-    for c, (_, size) in enumerate(chunks):
-        y_free = y_free + size
-        times.append((y_free, 0, c))
-        z_free = max(z_free, y_free) + size * (1.0 if c == 0 else 1.5)
-        times.append((z_free, 1, c))
-        mid_free = max(mid_free, z_free) + 2 * size
-        times.append((mid_free, 2, c))
-    return [(level, c) for _, level, c in sorted(times)]
+    size = 16
+    return tuple((start, size) for start in range(0, rows, size))
+
+
+def order_of(count):
+    steps = []
+    begun = 0
+    for c in range(count):
+        while begun < min(count, c + 2 + (c >= 2)):
+            steps.append((0, begun))
+            begun += 1
+        steps.append((1, c))
+        if c >= 2:
+            steps.append((2, c - 2))
+    return steps + [(2, c) for c in range(max(count - 2, 0), count)]
 
 
 def flip(index, step):
@@ -157,10 +155,12 @@
     load_x.wait()
     loaded = set()
     pending = []
-    for level, c in order_of(chunks):
+    for level, c in order_of(count):
         exchange(level, c).wait_recv()
-        if level == 0 and c + 1 < count:
-            exchange(0, c + 1).start()
+        if level == 0:
+            for later in (1, 2) if c == 0 else (c + 2,):
+                if later < count:
+                    exchange(0, later).start()
         if level not in loaded:
             for copy in loads[level]:
                 copy.wait()

time: 140 us -> 126 us (0.900)
  Pallas kernels: 138 us -> 123 us
    pallas_call x1, Pallas kernels: 138 us -> 123 us  [body(): pl.pallas_call(functools.partial(kernel, n_hi, n_lo, chunks), out_shape=j...]
where the time goes in v2:
time: 126 us; the launch traced here: 125 us
  Pallas kernels  123 us (98%)
  local copies, waits for them, and re-layouts  1.89 us (2%)
    pallas_call x1, Pallas kernels, body(): pl.pallas_call(functools.partial(kernel, n_hi, n_lo, chunks), out_shape=j...  123 us

profile of v2, /device:TPU:0, one launch (start us, length us, event | category | flops | bytes accessed | tf_op | source)
XLA Modules:
  0.0 125.3 jit_solution(14416713183593157365)
XLA Ops:
  0.0 123.4 %shard_map.46 = bf16[16,128,128]{2,1,0:T(8,128)(2,1)} custom-call(s32[4,64]{1,0:T(4,128)} %maps.1, bf16[64,128,128]{2,1,0:T(8,128)(2,1)} %blocks.1, bf16[4,64,128,128]{3,2,1,0:T(8,128)(2,1)} %diag.1, bf16[4,64,128,128]{3,2,1,0:T(8,128)(2,1)} %off.1), custom_call_target="tpu_custom_call" | custom-call | flops 2147483648 | bytes 19398656 | tf_op jit(solution)/shard_map/pallas_call | solution.py:201
  123.4 1.9 %copy.6 = bf16[16,128,128]{2,1,0:T(8,128)(2,1)} copy(bf16[16,128,128]{2,1,0:T(8,128)(2,1)} %shard_map.46) | data formatting | bytes 1048576

commit v3 on v2

--- a/solution.py
+++ b/solution.py
@@ -8,7 +8,7 @@
 from jax.sharding import PartitionSpec as P
 
 MESH = pl.DeviceIdType.MESH
-UNROLL = 16
+UNROLL = 8
 
 
 def chunk_plan(rows):
@@ -17,16 +17,19 @@
 
 
 def order_of(count):
-    steps = []
-    begun = 0
-    for c in range(count):
-        while begun < min(count, c + 2 + (c >= 2)):
-            steps.append((0, begun))
-            begun += 1
-        steps.append((1, c))
-        if c >= 2:
-            steps.append((2, c - 2))
-    return steps + [(2, c) for c in range(max(count - 2, 0), count)]
+    if count != 8:
+        return [(level, (c,)) for c in range(count) for level in range(3)]
+    return [
+        (0, (0,)), (0, (1,)), (1, (0,)), (0, (2,)), (1, (1,)), (0, (3,)), (1, (2,)),
+        (0, (4, 5)), (1, (3,)), (2, (0, 1)), (1, (4,)), (0, (6, 7)), (2, (2, 3)),
+        (1, (5,)), (1, (6,)), (1, (7,)), (2, (4, 5)), (2, (6,)), (2, (7,)),
+    ]
+
+
+def issue_after(count):
+    if count != 8:
+        return {c: (c + 1,) for c in range(count - 1)}
+    return {0: (1,), 1: (2,), 2: (3, 4), 3: (5, 6), 5: (7,)}
 
 
 def flip(index, step):
@@ -59,7 +62,12 @@
 
     near = sorted(set(steps))
     lo_partner = {s: flip(lo, s) for s in near}
-    hi_partner = [lax.rem(hi + d, n_hi) for d in range(1, n_hi)]
+    hi_partner = []
+    for d in range(1, n_hi):
+        other = hi
+        for bit in range(n_hi.bit_length() - 1):
+            other = flip(other, 1 << bit) if d >> bit & 1 else other
+        hi_partner.append(other)
     barrier = pltpu.get_barrier_semaphore()
     for s in near:
         pl.semaphore_signal(barrier, inc=1, device_id=(hi, lo_partner[s]), device_id_type=MESH)
@@ -78,14 +86,17 @@
         copy.start()
     pl.semaphore_wait(barrier, len(near) + n_hi - 1)
 
-    def exchange(level, c):
+    half = nblk // 2
+
+    def exchange(level, c, part):
         start, size = chunks[c]
-        source = blocks.at[:, pl.ds(start, size), :] if level == 0 else xs[level][c]
+        own = pl.ds(part * half, half)
+        source = blocks.at[own, pl.ds(start, size), :] if level == 0 else xs[level][c].at[own]
         return pltpu.make_async_remote_copy(
             src_ref=source,
-            dst_ref=recv[level][c],
-            send_sem=send_sem.at[level, c],
-            recv_sem=recv_sem.at[level, c],
+            dst_ref=recv[level][c].at[own],
+            send_sem=send_sem.at[level, c, part],
+            recv_sem=recv_sem.at[level, c, part],
             device_id=(hi, lo_partner[steps[level]]),
             device_id_type=MESH,
         )
@@ -100,44 +111,64 @@
             device_id_type=MESH,
         )
 
-    def product(left, right, d, o):
+    def product(pairs, d, o):
+        rows = [jnp.concatenate(pair, axis=1) for pair in pairs]
         return lax.dot_general(
-            jnp.concatenate([left, right], axis=1),
+            jnp.concatenate(rows, axis=0),
             jnp.concatenate([d, o], axis=1),
             (((1,), (1,)), ((), ())),
             preferred_element_type=jnp.float32,
         ).astype(jnp.bfloat16)
 
-    def over_blocks(number, one):
+    def over_blocks(first, number, one):
         unroll = UNROLL if number % UNROLL == 0 else 1
 
         def some(i, _):
             for u in range(unroll):
-                one(i * unroll + u)
+                one(first + i * unroll + u)
             return 0
 
         lax.fori_loop(0, number // unroll, some, 0)
 
-    def mix(level, c):
-        start, size = chunks[c]
-
+    def put(targets, j, cs, value):
+        row = 0
+        for c in cs:
+            size = chunks[c][1]
+            targets[c][j] = value[row:row + size]
+            row += size
+
+    def mix(level, cs):
         def one(j):
-            mine = x0[j, pl.ds(start, size), :] if level == 0 else xs[level][c][j]
-            theirs = recv[level][c][maps[level, j]]
-            xs[level + 1][c][j] = product(mine, theirs, dfs[level][j], ofs[level][j])
-
-        over_blocks(nblk, one)
-
-    def last(c):
+            pairs = []
+            for c in cs:
+                start, size = chunks[c]
+                mine = x0[j, pl.ds(start, size), :] if level == 0 else xs[level][c][j]
+                pairs.append((mine, recv[level][c][maps[level, j]]))
+            put(xs[level + 1], j, cs, product(pairs, dfs[level][j], ofs[level][j]))
+
+        if level == 2:
+            over_blocks(0, nblk, one)
+            return
+        for part in range(2):
+            over_blocks(part * half, half, one)
+            for c in cs:
+                exchange(level + 1, c, part).start()
+
+    def last(cs):
         def one(j):
             p = maps[3, j]
-            partial[c][j] = product(xs[3][c][j], xs[3][c][p], dfs[3][j], ofs[3][p])
-
-        over_blocks(nblk, one)
+            pairs = [(xs[3][c][j], xs[3][c][p]) for c in cs]
+            put(partial, j, cs, product(pairs, dfs[3][j], ofs[3][p]))
+
+        for d in range(n_hi - 2, -1, -1):
+            over_blocks(hi_partner[d] * share, share, one)
+            for c in cs:
+                hand_on(c, d).start()
+        over_blocks(hi * share, share, one)
 
     def gather_sum(c):
         start, size = chunks[c]
-        for d in range(n_hi - 1):
+        for d in range(n_hi - 2, -1, -1):
             hand_on(c, d).wait_recv()
 
         def one(i):
@@ -146,44 +177,46 @@
                 total = total + others[c][d, i].astype(jnp.float32)
             out[i, pl.ds(start, size), :] = total.astype(jnp.bfloat16)
 
-        over_blocks(share, one)
-
-    exchange(0, 0).start()
+        over_blocks(0, share, one)
+
+    for part in range(2):
+        exchange(0, 0, part).start()
     for k in range(1, 4):
         for copy in loads[k]:
             copy.start()
     load_x.wait()
+    issue = issue_after(count)
     loaded = set()
-    pending = []
-    for level, c in order_of(count):
-        exchange(level, c).wait_recv()
-        if level == 0:
-            for later in (1, 2) if c == 0 else (c + 2,):
-                if later < count:
-                    exchange(0, later).start()
+
+    def ready(level):
         if level not in loaded:
             for copy in loads[level]:
                 copy.wait()
             loaded.add(level)
-        mix(level, c)
-        if level < 2:
-            exchange(level + 1, c).start()
-            continue
-        if 3 not in loaded:
-            for copy in loads[3]:
-                copy.wait()
-            loaded.add(3)
-        last(c)
-        for d in range(n_hi - 1):
-            hand_on(c, d).start()
-        for earlier in pending:
-            gather_sum(earlier)
-        pending = [c]
+
+    pending = ()
+    for level, cs in order_of(count):
+        for c in cs:
+            for part in range(2):
+                exchange(level, c, part).wait_recv()
+            if level == 0:
+                for later in issue.get(c, ()):
+                    for part in range(2):
+                        exchange(0, later, part).start()
+        ready(level)
+        mix(level, cs)
+        if level == 2:
+            ready(3)
+            last(cs)
+            for earlier in pending:
+                gather_sum(earlier)
+            pending = cs
     for earlier in pending:
         gather_sum(earlier)
     for c in range(count):
         for level in range(3):
-            exchange(level, c).wait_send()
+            for part in range(2):
+                exchange(level, c, part).wait_send()
         for d in range(n_hi - 1):
             hand_on(c, d).wait_send()
 
@@ -206,8 +239,8 @@
         scratch_shapes=[whole] + pieces * 7 + shares + [factor] * 8 + [
             pltpu.SemaphoreType.DMA,
             pltpu.SemaphoreType.DMA((2, 4)),
-            pltpu.SemaphoreType.DMA((3, count)),
-            pltpu.SemaphoreType.DMA((3, count)),
+            pltpu.SemaphoreType.DMA((3, count, 2)),
+            pltpu.SemaphoreType.DMA((3, count, 2)),
             pltpu.SemaphoreType.DMA((n_hi - 1, count)),
             pltpu.SemaphoreType.DMA((n_hi - 1, count)),
         ],

time: 126 us -> 128 us (1.016)
  Pallas kernels: 123 us -> 126 us
    pallas_call x1, Pallas kernels: 123 us -> 126 us  [body(): pl.pallas_call(functools.partial(kernel, n_hi, n_lo, chunks), out_shape=j...]
where the time goes in v3:
time: 128 us
  Pallas kernels  126 us (98%)
  local copies, waits for them, and re-layouts  1.89 us (1%)
    pallas_call x1, Pallas kernels, body(): pl.pallas_call(functools.partial(kernel, n_hi, n_lo, chunks), out_shape=j...  126 us

profile of v3, /device:TPU:0, one launch (start us, length us, event | category | flops | bytes accessed | tf_op | source)
XLA Modules:
  0.0 127.5 jit_solution(10953632636017668249)
XLA Ops:
  0.0 125.6 %shard_map.46 = bf16[16,128,128]{2,1,0:T(8,128)(2,1)} custom-call(s32[4,64]{1,0:T(4,128)} %maps.1, bf16[64,128,128]{2,1,0:T(8,128)(2,1)} %blocks.1, bf16[4,64,128,128]{3,2,1,0:T(8,128)(2,1)} %diag.1, bf16[4,64,128,128]{3,2,1,0:T(8,128)(2,1)} %off.1), custom_call_target="tpu_custom_call" | custom-call | flops 2147483648 | bytes 19398656 | tf_op jit(solution)/shard_map/pallas_call | solution.py:234
  125.6 1.9 %copy.6 = bf16[16,128,128]{2,1,0:T(8,128)(2,1)} copy(bf16[16,128,128]{2,1,0:T(8,128)(2,1)} %shard_map.46) | data formatting | bytes 1048576

commit v4 on v3

--- a/solution.py
+++ b/solution.py
@@ -20,16 +20,16 @@
     if count != 8:
         return [(level, (c,)) for c in range(count) for level in range(3)]
     return [
-        (0, (0,)), (0, (1,)), (1, (0,)), (0, (2,)), (1, (1,)), (0, (3,)), (1, (2,)),
-        (0, (4, 5)), (1, (3,)), (2, (0, 1)), (1, (4,)), (0, (6, 7)), (2, (2, 3)),
-        (1, (5,)), (1, (6,)), (1, (7,)), (2, (4, 5)), (2, (6,)), (2, (7,)),
+        (0, (0,)), (0, (1,)), (1, (0,)), (0, (2,)), (1, (1,)), (0, (3,)), (0, (4,)),
+        (1, (2,)), (0, (5,)), (0, (6,)), (1, (3,)), (0, (7,)), (1, (4,)), (2, (0, 1)),
+        (1, (5,)), (1, (6,)), (2, (2, 3)), (1, (7,)), (2, (4, 5)), (2, (6,)), (2, (7,)),
     ]
 
 
 def issue_after(count):
     if count != 8:
         return {c: (c + 1,) for c in range(count - 1)}
-    return {0: (1,), 1: (2,), 2: (3, 4), 3: (5, 6), 5: (7,)}
+    return {0: (1,), 1: (2, 3), 2: (4,), 3: (5,), 4: (6,), 5: (7,)}
 
 
 def flip(index, step):

time: 128 us -> 126 us (0.984)
  Pallas kernels: 126 us -> 124 us
    pallas_call x1, Pallas kernels: 126 us -> 124 us  [body(): pl.pallas_call(functools.partial(kernel, n_hi, n_lo, chunks), out_shape=j...]
where the time goes in v4:
time: 126 us
  Pallas kernels  124 us (98%)
  local copies, waits for them, and re-layouts  1.89 us (2%)
    pallas_call x1, Pallas kernels, body(): pl.pallas_call(functools.partial(kernel, n_hi, n_lo, chunks), out_shape=j...  124 us

profile of v4, /device:TPU:0, one launch (start us, length us, event | category | flops | bytes accessed | tf_op | source)
XLA Modules:
  0.0 126.0 jit_solution(14612499463361695914)
XLA Ops:
  0.0 124.1 %shard_map.46 = bf16[16,128,128]{2,1,0:T(8,128)(2,1)} custom-call(s32[4,64]{1,0:T(4,128)} %maps.1, bf16[64,128,128]{2,1,0:T(8,128)(2,1)} %blocks.1, bf16[4,64,128,128]{3,2,1,0:T(8,128)(2,1)} %diag.1, bf16[4,64,128,128]{3,2,1,0:T(8,128)(2,1)} %off.1), custom_call_target="tpu_custom_call" | custom-call | flops 2147483648 | bytes 19398656 | tf_op jit(solution)/shard_map/pallas_call | solution.py:234
  124.1 1.9 %copy.6 = bf16[16,128,128]{2,1,0:T(8,128)(2,1)} copy(bf16[16,128,128]{2,1,0:T(8,128)(2,1)} %shard_map.46) | data formatting | bytes 1048576

commit v5 on v4

--- a/solution.py
+++ b/solution.py
@@ -8,7 +8,7 @@
 from jax.sharding import PartitionSpec as P
 
 MESH = pl.DeviceIdType.MESH
-UNROLL = 8
+UNROLL = 16
 
 
 def chunk_plan(rows):
@@ -120,12 +120,14 @@
             preferred_element_type=jnp.float32,
         ).astype(jnp.bfloat16)
 
-    def over_blocks(first, number, one):
+    def over_blocks(first, number, one, store):
         unroll = UNROLL if number % UNROLL == 0 else 1
 
         def some(i, _):
-            for u in range(unroll):
-                one(first + i * unroll + u)
+            group = [first + i * unroll + u for u in range(unroll)]
+            values = [one(j) for j in group]
+            for j, value in zip(group, values):
+                store(j, value)
             return 0
 
         lax.fori_loop(0, number // unroll, some, 0)
@@ -144,13 +146,16 @@
                 start, size = chunks[c]
                 mine = x0[j, pl.ds(start, size), :] if level == 0 else xs[level][c][j]
                 pairs.append((mine, recv[level][c][maps[level, j]]))
-            put(xs[level + 1], j, cs, product(pairs, dfs[level][j], ofs[level][j]))
+            return product(pairs, dfs[level][j], ofs[level][j])
+
+        def store(j, value):
+            put(xs[level + 1], j, cs, value)
 
         if level == 2:
-            over_blocks(0, nblk, one)
+            over_blocks(0, nblk, one, store)
             return
         for part in range(2):
-            over_blocks(part * half, half, one)
+            over_blocks(part * half, half, one, store)
             for c in cs:
                 exchange(level + 1, c, part).start()
 
@@ -158,13 +163,16 @@
         def one(j):
             p = maps[3, j]
             pairs = [(xs[3][c][j], xs[3][c][p]) for c in cs]
-            put(partial, j, cs, product(pairs, dfs[3][j], ofs[3][p]))
+            return product(pairs, dfs[3][j], ofs[3][p])
+
+        def store(j, value):
+            put(partial, j, cs, value)
 
         for d in range(n_hi - 2, -1, -1):
-            over_blocks(hi_partner[d] * share, share, one)
+            over_blocks(hi_partner[d] * share, share, one, store)
             for c in cs:
                 hand_on(c, d).start()
-        over_blocks(hi * share, share, one)
+        over_blocks(hi * share, share, one, store)
 
     def gather_sum(c):
         start, size = chunks[c]
@@ -175,9 +183,12 @@
             total = partial[c][hi * share + i].astype(jnp.float32)
             for d in range(n_hi - 1):
                 total = total + others[c][d, i].astype(jnp.float32)
-            out[i, pl.ds(start, size), :] = total.astype(jnp.bfloat16)
-
-        over_blocks(0, share, one)
+            return total.astype(jnp.bfloat16)
+
+        def store(i, value):
+            out[i, pl.ds(start, size), :] = value
+
+        over_blocks(0, share, one, store)
 
     for part in range(2):
         exchange(0, 0, part).start()

time: 126 us -> 124 us (0.984)
  Pallas kernels: 124 us -> 122 us
    pallas_call x1, Pallas kernels: 124 us -> 122 us  [body(): pl.pallas_call(functools.partial(kernel, n_hi, n_lo, chunks), out_shape=j...]
where the time goes in v5:
time: 124 us
  Pallas kernels  122 us (98%)
  local copies, waits for them, and re-layouts  1.89 us (2%)
    pallas_call x1, Pallas kernels, body(): pl.pallas_call(functools.partial(kernel, n_hi, n_lo, chunks), out_shape=j...  122 us

profile of v5, /device:TPU:0, one launch (start us, length us, event | category | flops | bytes accessed | tf_op | source)
XLA Modules:
  0.0 124.1 jit_solution(7413583078576892363)
XLA Ops:
  0.0 122.2 %shard_map.46 = bf16[16,128,128]{2,1,0:T(8,128)(2,1)} custom-call(s32[4,64]{1,0:T(4,128)} %maps.1, bf16[64,128,128]{2,1,0:T(8,128)(2,1)} %blocks.1, bf16[4,64,128,128]{3,2,1,0:T(8,128)(2,1)} %diag.1, bf16[4,64,128,128]{3,2,1,0:T(8,128)(2,1)} %off.1), custom_call_target="tpu_custom_call" | custom-call | flops 2147483648 | bytes 19398656 | tf_op jit(solution)/shard_map/pallas_call | solution.py:245
  122.2 1.9 %copy.6 = bf16[16,128,128]{2,1,0:T(8,128)(2,1)} copy(bf16[16,128,128]{2,1,0:T(8,128)(2,1)} %shard_map.46) | data formatting | bytes 1048576

commit v6 on v5

--- a/solution.py
+++ b/solution.py
@@ -115,8 +115,8 @@
         rows = [jnp.concatenate(pair, axis=1) for pair in pairs]
         return lax.dot_general(
             jnp.concatenate(rows, axis=0),
-            jnp.concatenate([d, o], axis=1),
-            (((1,), (1,)), ((), ())),
+            jnp.concatenate([d, o], axis=0),
+            (((1,), (0,)), ((), ())),
             preferred_element_type=jnp.float32,
         ).astype(jnp.bfloat16)
 
@@ -131,6 +131,18 @@
             return 0
 
         lax.fori_loop(0, number // unroll, some, 0)
+
+    def turn(level):
+        unroll = 4 if nblk % 4 == 0 else 1
+
+        def some(i, _):
+            for u in range(unroll):
+                j = i * unroll + u
+                dfs[level][j] = dfs[level][j].T
+                ofs[level][j] = ofs[level][j].T
+            return 0
+
+        lax.fori_loop(0, nblk // unroll, some, 0)
 
     def put(targets, j, cs, value):
         row = 0
@@ -204,7 +216,9 @@
             for copy in loads[level]:
                 copy.wait()
             loaded.add(level)
-
+            turn(level)
+
+    ready(0)
     pending = ()
     for level, cs in order_of(count):
         for c in cs:
@@ -216,6 +230,9 @@
                         exchange(0, later, part).start()
         ready(level)
         mix(level, cs)
+        early = {(0, 0): 1, (1, 1): 2, (1, 3): 3}.get((level, cs[0]))
+        if early is not None:
+            ready(early)
         if level == 2:
             ready(3)
             last(cs)

time: 124 us -> 123 us (level)
  no operation moved by 1% of the time
where the time goes in v6:
time: 123 us
  Pallas kernels  121 us (98%)
  local copies, waits for them, and re-layouts  1.89 us (2%)
    pallas_call x1, Pallas kernels, body(): pl.pallas_call(functools.partial(kernel, n_hi, n_lo, chunks), out_shape=j...  121 us

profile of v6, /device:TPU:0, one launch (start us, length us, event | category | flops | bytes accessed | tf_op | source)
XLA Modules:
  0.0 122.9 jit_solution(15511580741083580189)
XLA Ops:
  0.0 121.0 %shard_map.46 = bf16[16,128,128]{2,1,0:T(8,128)(2,1)} custom-call(s32[4,64]{1,0:T(4,128)} %maps.1, bf16[64,128,128]{2,1,0:T(8,128)(2,1)} %blocks.1, bf16[4,64,128,128]{3,2,1,0:T(8,128)(2,1)} %diag.1, bf16[4,64,128,128]{3,2,1,0:T(8,128)(2,1)} %off.1), custom_call_target="tpu_custom_call" | custom-call | flops 2147483648 | bytes 19398656 | tf_op jit(solution)/shard_map/pallas_call | solution.py:262
  121.0 1.9 %copy.6 = bf16[16,128,128]{2,1,0:T(8,128)(2,1)} copy(bf16[16,128,128]{2,1,0:T(8,128)(2,1)} %shard_map.46) | data formatting | bytes 1048576
